TPU v7x, 32 devices: a whole 2x2x4 slice. The times are simulated.
32 devices in a mesh: row: 8 (over y, x, core), col: 4 (over z).
Axes of the slice: x: 2, y: 2, z: 4, core: 2. Of those that a mesh axis runs over, the one named last changes fastest.
Arguments:
- band_cells: float32 [3, 256, 2], P(None, ('row', 'col')), may hold values from 0 to 1
- cell_counts: int32 [256], P(('row', 'col')), may hold values from 1 to 2, as said below
- cell_assign: int32 [256], P(('row', 'col')), may hold values from 0 to 255, as said below
- wake_pos: float32 [3, 262144], P(None, ('row', 'col')), may hold values from 0 to 1
- wake_strength: float32 [3, 262144], P(None, ('row', 'col')), may hold values from -0.01171875 to 0.01171875
- wake_core: float32 [1, 262144], P(None, ('row', 'col')), may hold values from 0.05 to 0.15
Outputs:
- velocity: float32 [3, 256, 2], P(None, ('row', 'col'))
- gradient: float32 [9, 256, 2], P(None, ('row', 'col'))
Inputs may be any that keep to these rules, and one draw needn't show every extreme that they name: `cell_counts`: each band cell holds its live particles in its first slots; some cell is full in every draw. `cell_assign`: A permutation of the cells. The cells of the device with index d along row+col go to positions q with q // 32 == d // 4; at most 2 of them land in the positions of any one device (q // 8); where 8 is a multiple of 4, exactly 2 land in the positions of each device of the group, else some pair of devices reaches 2.
All inputs are finite; a program needn't handle non-finite values.
Results may differ from a plain program's by a relative error of at most 0.0003.
Values sent between devices are 32-bit elements; how exact they have to be, the bound alone decides.
A program may use at most 64 MiB of HBM per device.

v0:
```python
import math

import jax
import jax.numpy as jnp
from jax import lax
from jax.sharding import PartitionSpec as P

HIGHEST = lax.Precision.HIGHEST


def block_sums(target_pos, source_pos, source_str, source_core):
    delta_x = target_pos[0][:, None] - source_pos[0][None, :]
    delta_y = target_pos[1][:, None] - source_pos[1][None, :]
    delta_z = target_pos[2][:, None] - source_pos[2][None, :]
    radius_sq = (
        delta_x * delta_x
        + delta_y * delta_y
        + delta_z * delta_z
        + source_core[0][None, :] * source_core[0][None, :]
    )
    inverse = lax.rsqrt(radius_sq)
    kernel_three = inverse * inverse * inverse
    kernel_five = kernel_three * inverse * inverse
    alpha_x = source_str[0][None, :]
    alpha_y = source_str[1][None, :]
    alpha_z = source_str[2][None, :]
    cross_x = delta_y * alpha_z - delta_z * alpha_y
    cross_y = delta_z * alpha_x - delta_x * alpha_z
    cross_z = delta_x * alpha_y - delta_y * alpha_x
    terms_list = [
        kernel_three * cross_x,
        kernel_three * cross_y,
        kernel_three * cross_z,
        kernel_three * alpha_x,
        kernel_three * alpha_y,
        kernel_three * alpha_z,
    ]
    for along in (delta_x, delta_y, delta_z):
        for cross in (cross_x, cross_y, cross_z):
            terms_list.append(kernel_five * along * cross)
    return jnp.stack([jnp.sum(term, axis=1) for term in terms_list])


def pair_sums(target_pos, source_pos, source_str, source_core):
    source_total = source_pos.shape[1]
    block_width = math.gcd(source_total, max(512, 1048576 // target_pos.shape[1]))
    block_steps = source_total // block_width

    def one_block(running, block_index):
        offset = block_index * block_width
        part_pos = lax.dynamic_slice_in_dim(source_pos, offset, block_width, 1)
        part_str = lax.dynamic_slice_in_dim(source_str, offset, block_width, 1)
        part_core = lax.dynamic_slice_in_dim(source_core, offset, block_width, 1)
        return (running + block_sums(target_pos, part_pos, part_str, part_core), None)

    start_sums = jnp.zeros((15, target_pos.shape[1]), jnp.float32)
    running, unused = lax.scan(one_block, start_sums, jnp.arange(block_steps, dtype=jnp.int32))
    return running


def combine_rows(kernel_sums):
    biot_scale = -1.0 / (4.0 * math.pi)
    swirl_x, swirl_y, swirl_z = (kernel_sums[3], kernel_sums[4], kernel_sums[5])
    zero_row = jnp.zeros_like(swirl_x)
    levi_terms = [
        [zero_row, swirl_z, -swirl_y],
        [-swirl_z, zero_row, swirl_x],
        [swirl_y, -swirl_x, zero_row],
    ]
    out_rows = [
        biot_scale * kernel_sums[0],
        biot_scale * kernel_sums[1],
        biot_scale * kernel_sums[2],
    ]
    for comp_m in range(3):
        for comp_n in range(3):
            out_rows.append(
                biot_scale
                * (levi_terms[comp_m][comp_n] - 3.0 * kernel_sums[6 + comp_n * 3 + comp_m])
            )
    return jnp.stack(out_rows)


def apply_mask(finished_rows, slot_counts, slot_cap):
    slot_ids = jnp.arange(slot_cap).astype(slot_counts.dtype)
    alive_mask = (slot_ids[None, :] < slot_counts[:, None]).astype(jnp.float32).reshape(-1)
    masked = finished_rows * alive_mask[None, :]
    cell_total = slot_counts.shape[0]
    return (
        masked[0:3].reshape(3, cell_total, slot_cap),
        masked[3:12].reshape(9, cell_total, slot_cap),
    )


def per_device(band_cells, cell_counts, cell_assign, wake_pos, wake_strength, wake_core):
    col_devs = lax.axis_size("col")
    cell_total = band_cells.shape[1]
    slot_cap = band_cells.shape[2]
    block_cells = cell_total * col_devs
    counts_float = cell_counts.astype(jnp.float32)
    band_block, band_counts, band_assign = (
        lax.all_gather(band_cells, "col", axis=1, tiled=True),
        lax.all_gather(counts_float, "col", axis=0, tiled=True),
        lax.all_gather(cell_assign.astype(jnp.float32), "col", axis=0, tiled=True),
    )
    local_order = band_assign.astype(jnp.int32) % block_cells
    reorder_map = (
        local_order[None, :] == jnp.arange(block_cells, dtype=jnp.int32)[:, None]
    ).astype(jnp.float32)
    target_block = jnp.einsum("qt,ftc->fqc", reorder_map, band_block, precision=HIGHEST)
    block_counts = jnp.dot(reorder_map, band_counts, precision=HIGHEST)
    own_counts = lax.dynamic_slice_in_dim(
        block_counts, lax.axis_index("col") * cell_total, cell_total
    )
    target_pos = target_block.reshape(3, -1)
    local_sums = pair_sums(
        target_pos,
        lax.all_gather(wake_pos, "row", axis=1, tiled=True),
        lax.all_gather(wake_strength, "row", axis=1, tiled=True),
        lax.all_gather(wake_core, "row", axis=1, tiled=True),
    )
    own_rows = lax.psum_scatter(local_sums, "col", scatter_dimension=1, tiled=True)
    finished_rows = combine_rows(own_rows)
    return apply_mask(finished_rows, own_counts, slot_cap)


def solution(mesh):
    placed = (
        P(None, ("row", "col"), None),
        P(("row", "col")),
        P(("row", "col")),
        P(None, ("row", "col")),
        P(None, ("row", "col")),
        P(None, ("row", "col")),
    )
    return jax.shard_map(
        per_device,
        mesh=mesh,
        in_specs=placed,
        out_specs=(P(None, ("row", "col"), None), P(None, ("row", "col"), None)),
        check_vma=False,
    )
```

profile of v0, /device:TPU:0, one launch (start us, length us, event | category | flops | bytes accessed | tf_op | source)
XLA Modules:
  0.0 149.3 jit_solution(9550363035874051836)
XLA Ops:
  7.2 0.0 copy-start
  7.2 0.0 reduce-scatter.4.cloned.1.call-start
  7.2 1.2 dynamic-slice
  9.1 0.8 convert_dynamic-update-slice_fusion.1
  9.9 0.7 convert_dynamic-update-slice_fusion
  10.6 13.4 %all-reduce.2 = (f32[32]{0:T(128)S(1)}, f32[32]{0:T(128)S(1)}) all-reduce(f32[32]{0:T(128)S(1)} %convert_dynamic-update-slice_fusion.1, f32[32]{0:T(128)S(1)} %convert_dynamic-update-slice_fusion), channel_id=1, replica_groups=mesh['row'=8,'col'=4] {'col'}, use_global_device_ids=true, to_apply=%add | all-reduce | flops 64 | bytes 512
  24.1 0.8 copy.40
  24.9 13.1 %all_gather.19 = f32[3,32,2]{0,2,1:T(2,128)S(1)} all-gather(f32[3,8,2]{0,2,1:T(2,128)S(1)} %copy.40), channel_id=1, replica_groups=mesh['row'=8,'col'=4] {'col'}, dimensions={1}, use_global_device_ids=true | all-gather | bytes 960 | tf_op jit(solution)/shard_map/all_gather | solution.py:102
  38.0 0.2 convolution_bitcast_fusion
  38.2 0.1 copy.42
  38.3 0.1 reshape.41
  38.4 9.5 %all_gather.21 = f32[1,65536]{1,0:T(1,128)S(1)} all-gather(f32[1,8192]{1,0:T(1,128)} %param.13), channel_id=1, replica_groups=mesh['row'=8,'col'=4] {'row'}, dimensions={1}, use_global_device_ids=true | all-gather | bytes 294912 | tf_op jit(solution)/shard_map/all_gather | solution.py:120
  47.9 11.1 %all_gather.20 = f32[3,65536]{1,0:T(4,128)S(1)} all-gather(f32[3,8192]{1,0:T(4,128)} %param.11), channel_id=1, replica_groups=mesh['row'=8,'col'=4] {'row'}, dimensions={1}, use_global_device_ids=true | all-gather | bytes 884736 | tf_op jit(solution)/shard_map/all_gather | solution.py:118
  59.0 0.0 copy-done
  59.0 11.2 %all_gather.22 = f32[3,65536]{1,0:T(4,128)S(1)} all-gather(f32[3,8192]{1,0:T(4,128)S(1)} %copy-done), channel_id=1, replica_groups=mesh['row'=8,'col'=4] {'row'}, dimensions={1}, use_global_device_ids=true | all-gather | bytes 884736 | tf_op jit(solution)/shard_map/all_gather | solution.py:119
  70.1 52.4 %while.11 = (s32[]{:T(128)}, f32[15,64]{1,0:T(8,128)S(1)}, f32[3,64]{1,0:T(4,128)S(1)}, s32[4]{0:T(128)S(1)}, f32[3,65536]{1,0:T(4,128)S(1)}, /*index=5*/f32[1,6...) while((s32[]{:T(128)}, f32[15,64]{1,0:T(8,128)S(1)}, ...), condition=%wide.region_16.17_spmd.clone, body=%wide.region_0.16_spmd.clone.sunk | while | flops 57689032 | bytes 1401849 | solution.py:57
  70.1 0.6 dynamic_slice.23
  71.4 0.3 fusion.59
  71.7 0.4 constant_dynamic-slice_fusion.3
  72.1 11.1 %fusion.60 = (f32[64]{0:T(128)S(1)}, f32[64]{0:T(128)S(1)}, f32[64]{0:T(128)S(1)}, f32[64]{0:T(128)S(1)}, f32[64]{0:T(128)S(1)}, /*index=5*/f32[64]{0:T(128)S(1)...) fusion(f32[16384]{0:T(1024)S(1)} %bitcast.100, ...), kind=kLoop, calls=%fused_computation.28.clone.1 | loop fusion | flops 57670720 | bytes 463360 | tf_op jit(solution)/shard_map/while/body/eval_jaxpr/reduce_sum | solution.py:41
  83.3 0.6 dynamic_slice.23
  84.5 0.3 fusion.59
  84.9 0.4 constant_dynamic-slice_fusion.3
  85.2 11.1 %fusion.60 = (f32[64]{0:T(128)S(1)}, f32[64]{0:T(128)S(1)}, f32[64]{0:T(128)S(1)}, f32[64]{0:T(128)S(1)}, f32[64]{0:T(128)S(1)}, /*index=5*/f32[64]{0:T(128)S(1)...) fusion(f32[16384]{0:T(1024)S(1)} %bitcast.100, ...), kind=kLoop, calls=%fused_computation.28.clone.1 | loop fusion | flops 57670720 | bytes 463360 | tf_op jit(solution)/shard_map/while/body/eval_jaxpr/reduce_sum | solution.py:41
  96.4 0.6 dynamic_slice.23
  97.6 0.3 fusion.59
  98.0 0.4 constant_dynamic-slice_fusion.3
  98.3 11.1 %fusion.60 = (f32[64]{0:T(128)S(1)}, f32[64]{0:T(128)S(1)}, f32[64]{0:T(128)S(1)}, f32[64]{0:T(128)S(1)}, f32[64]{0:T(128)S(1)}, /*index=5*/f32[64]{0:T(128)S(1)...) fusion(f32[16384]{0:T(1024)S(1)} %bitcast.100, ...), kind=kLoop, calls=%fused_computation.28.clone.1 | loop fusion | flops 57670720 | bytes 463360 | tf_op jit(solution)/shard_map/while/body/eval_jaxpr/reduce_sum | solution.py:41
  109.5 0.6 dynamic_slice.23
  110.7 0.3 fusion.59
  111.1 0.4 constant_dynamic-slice_fusion.3
  111.4 11.1 %fusion.60 = (f32[64]{0:T(128)S(1)}, f32[64]{0:T(128)S(1)}, f32[64]{0:T(128)S(1)}, f32[64]{0:T(128)S(1)}, f32[64]{0:T(128)S(1)}, /*index=5*/f32[64]{0:T(128)S(1)...) fusion(f32[16384]{0:T(1024)S(1)} %bitcast.100, ...), kind=kLoop, calls=%fused_computation.28.clone.1 | loop fusion | flops 57670720 | bytes 463360 | tf_op jit(solution)/shard_map/while/body/eval_jaxpr/reduce_sum | solution.py:41
  122.6 0.7 copy.62
  123.3 0.0 reduce-scatter.4.cloned.1.call-update
  123.3 0.1 convolution_bitcast_fusion.1
  123.4 0.1 dynamic_slice.16
  123.5 0.1 compare_convert_fusion
  123.6 0.1 reshape.44
  123.7 16.0 %reduce-scatter.4.cloned.1.call-done = f32[16,15]{1,0:T(8,128)} async-done(((f32[64,15]{1,0:T(8,128)}), f32[16,15]{1,0:T(8,128)}) %reduce-scatter.4.cloned.1.call-update) | async-done | bytes 976
  139.6 1.3 fusion.35
  140.9 0.1 stack.63
  141.0 0.1 broadcast_multiply_fusion
  141.1 0.7 slice.120
  141.8 0.7 copy.59
  (18 shorter events, 0.3 us)
Async XLA Ops:
  7.2 51.8 %copy-start = (f32[3,8192]{1,0:T(4,128)S(1)}, f32[3,8192]{1,0:T(4,128)}, u32[]{:S(2)}) copy-start(f32[3,8192]{1,0:T(4,128)} %param.12) | copy-start | bytes 294916
  7.2 132.4 %reduce-scatter.4.cloned.1.call-start = ((), (), s32[]{:S(2)}) async-start(), calls=%async_computation.1 | async-start | bytes 40960
Sparse Core Ops, SparseCore 0:
  123.4 16.1 reduce-scatter.3
where the time goes:
time: 150 us; the launch traced here: 149 us
  blocking collectives  58.3 us (39%)
  other arithmetic  48.7 us (32%)
  waiting for transfers between devices  16 us (11%)
  between operations  14.8 us (10%)
  local copies, waits for them, and re-layouts  8.47 us (6%)
  loops' own time  2.78 us (2%)
    reduce_sum x4, other arithmetic, block_sums(): return jnp.stack([jnp.sum(term, axis=1) for term in terms_list])  44.2 us
    unnamed x2, waiting for transfers between devices  16 us
    unnamed x1, blocking collectives  13.4 us
    all_gather x1, blocking collectives, per_device(): lax.all_gather(band_cells, 'col', axis=1, tiled=True)  13.1 us
    all_gather x1, blocking collectives, per_device(): lax.all_gather(wake_strength, 'row', axis=1, tiled=True)  11.2 us
    all_gather x1, blocking collectives, per_device(): lax.all_gather(wake_pos, 'row', axis=1, tiled=True)  11.1 us
    all_gather x1, blocking collectives, per_device(): lax.all_gather(wake_core, 'row', axis=1, tiled=True)  9.53 us
    unnamed x8, local copies, waits for them, and re-layouts  3.38 us
  transfers between devices with their start and end apart: 1, of which 1 were waited for; matrix products, arithmetic and copies ran while one was open for 0% of the time, Pallas kernels for 0%

commit v1 on v0

v1 whole, which is shorter than its diff:
```python
import functools
import math

import jax
import jax.numpy as jnp
from jax import lax
from jax.experimental import pallas as pl
from jax.experimental.pallas import tpu as pltpu
from jax.sharding import PartitionSpec as P

MESH = pl.DeviceIdType.MESH
LANES = 128
SUB = 8
CHUNK = 512
PREPARE = 1024
ROWS = 512
STRIP = 32
DEPTH = 48
CENTRE = 0.5


def split_three(value):
    high = value.astype(jnp.bfloat16).astype(jnp.float32)
    rest = value - high
    middle = rest.astype(jnp.bfloat16).astype(jnp.float32)
    return high, middle, rest - middle


def kernel(
    grid_rows, grid_cols,
    band_hbm, counts_hbm, assign_hbm, pos_hbm, str_hbm, core_hbm,
    inbox,
    band_ref, counts_ref, assign_ref, pos_ref, str_ref, core_ref, fetch,
    even, odd, note, notes, turned, place, left, source, weights, sums, parcel, own,
    note_send, note_recv, parcel_send, parcel_recv,
):
    total = grid_rows * grid_cols
    slots, cells = band_ref.shape[1:]
    block = cells * grid_cols
    width = note.shape[2] // slots
    held = cells * slots
    targets = total * held
    me_row = lax.axis_index("row")
    me_col = lax.axis_index("col")
    me = me_row * grid_cols + me_col

    fetches = [
        pltpu.make_async_copy(far, near, fetch.at[i])
        for i, (far, near) in enumerate(
            [
                (assign_hbm, assign_ref), (band_hbm, band_ref), (counts_hbm, counts_ref),
                (pos_hbm, pos_ref), (str_hbm, str_ref), (core_hbm, core_ref),
            ]
        )
    ]
    for one in fetches:
        one.start()

    def each_other(act):
        others = [lax.rem(me_col + z, grid_cols) for z in range(grid_cols)]
        for z in range(1, grid_cols):
            act((me_row, others[z]), me_row * grid_cols + others[z])

        def in_row(step, unused):
            there = lax.rem(me_row + step, grid_rows)
            for z in range(grid_cols):
                act((there, others[z]), there * grid_cols + others[z])
            return unused

        lax.fori_loop(1, grid_rows, in_row, 0)

    barrier = pltpu.get_barrier_semaphore()

    def greet(there, other):
        pl.semaphore_signal(barrier, inc=1, device_id=there, device_id_type=MESH)

    each_other(greet)

    for one in fetches[:3]:
        one.wait()
    lane = lax.broadcasted_iota(jnp.int32, (cells, width), 1)
    row = lax.broadcasted_iota(jnp.int32, (cells, width), 0)
    position = jnp.zeros((cells, width), jnp.int32)
    live = jnp.zeros((cells, width), jnp.float32)
    columns = [[jnp.zeros((cells, width), jnp.float32)] * slots for k in range(3)]
    for t in range(cells):
        for k in range(3):
            for s in range(slots):
                columns[k][s] = jnp.where(row == t, band_ref[k, s, t], columns[k][s])
        position = jnp.where(row == t, lax.rem(assign_ref[t], block), position)
        live = jnp.where(row == t, counts_ref[t].astype(jnp.float32), live)
    chosen = lax.rem(lane, block) == position
    kind = lane // block
    for s in range(slots):
        value = jnp.where(kind == 3, live, 0.0)
        for k in range(3):
            value = jnp.where(kind == k, columns[k][s] - CENTRE, value)
        value = jnp.where(chosen, value, 0.0)
        note[0, :, s * width : (s + 1) * width] = jnp.sum(value, axis=0, keepdims=True)

    pl.semaphore_wait(barrier, total - 1)

    def tell(there, other):
        pltpu.make_async_remote_copy(
            src_ref=note.at[0], dst_ref=notes.at[me], send_sem=note_send, recv_sem=note_recv,
            device_id=there, device_id_type=MESH,
        ).start()

    each_other(tell)
    notes[me] = note[0]

    for one in fetches[3:]:
        one.wait()
    span = source.shape[1]

    def prepare(index, unused):
        cols = pl.ds(pl.multiple_of(index * PREPARE, PREPARE), PREPARE)
        ys = [pos_ref[k : k + 1, cols] - CENTRE for k in range(3)]
        al = [str_ref[k : k + 1, cols] for k in range(3)]
        core = core_ref[0:1, cols]
        core_sq = core * core
        norm = ys[0] * ys[0] + ys[1] * ys[1] + ys[2] * ys[2] + core_sq
        be = [
            ys[(m + 1) % 3] * al[(m + 2) % 3] - ys[(m + 2) % 3] * al[(m + 1) % 3]
            for m in range(3)
        ]
        ones = jnp.ones((1, PREPARE), jnp.float32)
        blank = jnp.zeros((3, PREPARE), jnp.float32)
        one, two, three = split_three(jnp.concatenate(ys + [norm, ones, blank], axis=0))
        source[:, cols] = jnp.concatenate([one, one, one, two, two, three], axis=0).astype(
            jnp.bfloat16
        )
        pad = jnp.zeros((2, PREPARE), jnp.float32)
        base = jnp.concatenate(al + be + [pad], axis=0)
        split = [split_three(base)] + [split_three(base * g) for g in ys + [norm]]
        rows = [split[b][j] for j in range(3) for b in range(5)]
        rows.append(jnp.zeros((SUB, PREPARE), jnp.float32))
        weights[:, cols] = jnp.concatenate(rows, axis=0).astype(jnp.bfloat16)
        return unused

    lax.fori_loop(0, span // PREPARE, prepare, 0)

    pltpu.make_async_copy(
        notes.at[pl.ds(0, total - 1)], notes.at[pl.ds(0, total - 1)], note_recv
    ).wait()
    turned[...] = jnp.zeros_like(turned)
    for g in range(grid_rows):
        merged = notes[g * grid_cols]
        for z in range(1, grid_cols):
            merged = merged + notes[g * grid_cols + z]
        for s in range(slots):
            turned[g * slots + s : g * slots + s + 1, :] = merged[:, s * width : (s + 1) * width]
    columns = jnp.concatenate(
        [turned[:, w : w + LANES].T for w in range(0, width, LANES)], axis=0
    )
    for g in range(grid_rows):
        for z in range(grid_cols):
            for s in range(slots):
                at = ((g * grid_cols + z) * slots + s) * cells
                for k in range(4):
                    low = k * block + z * cells
                    column = columns[low : low + cells, g * slots + s : g * slots + s + 1]
                    wide = jnp.broadcast_to(column, (cells, LANES))
                    if k == 3:
                        wide = jnp.where(wide > s + 0.5, 1.0, 0.0)
                    place[k, at : at + cells, :] = wide

    def sides(index, unused):
        rows = pl.ds(pl.multiple_of(index * LANES, LANES), LANES)
        lane = lax.broadcasted_iota(jnp.int32, (LANES, LANES), 1)
        xs = [place[k, rows, :] for k in range(3)]
        value = jnp.where(lane % SUB == 3, 1.0, 0.0)
        value = jnp.where(
            lane % SUB == 4, xs[0] * xs[0] + xs[1] * xs[1] + xs[2] * xs[2], value
        )
        for k in range(3):
            value = jnp.where(lane % SUB == k, -2.0 * xs[k], value)
        one, two, three = split_three(value)
        part = lane // SUB
        value = jnp.where((part == 1) | (part == 4), two, jnp.where(part == 2, three, one))
        left[rows, :] = jnp.where(part < 6, value, 0.0).astype(jnp.bfloat16)
        return unused

    lax.fori_loop(0, targets // LANES, sides, 0)

    sums[...] = jnp.zeros_like(sums)

    parts = targets // ROWS
    steps = (span // CHUNK) * parts

    def where_at(index):
        cols = pl.ds(pl.multiple_of((index // parts) * CHUNK, CHUNK), CHUNK)
        first = lax.rem(index, parts) * ROWS
        return cols, first

    def powers(index, store):
        cols, first = where_at(index)

        rows = pl.ds(pl.multiple_of(first, ROWS), ROWS)
        radius = jnp.dot(
            left[rows, 0:DEPTH], source[:, cols], preferred_element_type=jnp.float32
        )
        for low in range(0, ROWS, STRIP):
            inverse = lax.rsqrt(radius[low : low + STRIP])
            square = inverse * inverse
            power = square * square * inverse
            high = power.astype(jnp.bfloat16)
            rest = (power - high.astype(jnp.float32)).astype(jnp.bfloat16)
            store[low : low + STRIP, 0:CHUNK] = high
            store[low : low + STRIP, CHUNK : 2 * CHUNK] = rest

    def add(index, store):
        cols, first = where_at(index)
        rows = pl.ds(pl.multiple_of(first, ROWS), ROWS)
        both = jnp.concatenate([weights[:, cols]] * 2, axis=1)
        sums[rows, :] += lax.dot_general(
            store[...], both, (((1,), (1,)), ((), ())), preferred_element_type=jnp.float32
        )

    powers(0, even)

    def pairs(count, unused):
        index = 2 * count
        add(index, even)
        powers(index + 1, odd)
        add(index + 1, odd)
        powers(index + 2, even)
        return unused

    lax.fori_loop(0, steps // 2 - 1, pairs, 0)
    add(steps - 2, even)
    powers(steps - 1, odd)
    add(steps - 1, odd)

    scale = -1.0 / (4.0 * math.pi)
    lane = lax.broadcasted_iota(jnp.int32, (LANES, LANES), 1)
    sub = lax.broadcasted_iota(jnp.int32, (SUB, LANES), 0)
    group = lax.broadcasted_iota(jnp.int32, (SUB, LANES), 1) // held
    for i in range(targets // LANES):
        rows = slice(i * LANES, (i + 1) * LANES)
        tile = sums[rows, :]
        for k in range(4):
            tile = jnp.where(lane == 120 + k, place[k, rows, :], tile)
        tile = tile.T
        moment = [
            tile[b * SUB : (b + 1) * SUB]
            + (tile[40 + b * SUB : 48 + b * SUB] + tile[80 + b * SUB : 88 + b * SUB])
            for b in range(5)
        ]
        xs = [tile[120 + k : 121 + k] for k in range(3)]
        alive = tile[123:124]
        norm = xs[0] * xs[0] + xs[1] * xs[1] + xs[2] * xs[2]
        swirl = norm * moment[0] + moment[4]
        for n in range(3):
            swirl = swirl - (2.0 * xs[n]) * moment[1 + n]

        def cross(table):
            return [
                xs[(m + 1) % 3] * table[(m + 2) % 3 : (m + 2) % 3 + 1]
                - xs[(m + 2) % 3] * table[(m + 1) % 3 : (m + 1) % 3 + 1]
                - table[3 + m : 4 + m]
                for m in range(3)
            ]

        finished = cross(swirl)
        along = [cross(xs[n] * moment[0] - moment[1 + n]) for n in range(3)]
        for m in range(3):
            for n in range(3):
                term = -3.0 * along[n][m]
                if m != n:
                    other = 3 - m - n
                    part = swirl[other : other + 1]
                    term = term + part if (n - m) % 3 == 1 else term - part
                finished.append(term)
        zero = jnp.zeros((4, LANES), jnp.float32)
        packed = jnp.concatenate(finished + [zero], axis=0) * (alive * scale)
        for h in range(2):
            half = packed[h * SUB : (h + 1) * SUB]
            swapped = jnp.zeros((SUB, LANES), jnp.float32)
            for d in range(SUB):
                moved = half if d == 0 else pltpu.roll(half, d * held, 1)
                moved = jnp.where(group == sub, moved, 0.0)
                swapped = swapped + (moved if d == 0 else pltpu.roll(moved, SUB - d, 0))
            for j in range(SUB):
                parcel[i * SUB + j, :, h * LANES : (h + 1) * LANES] = swapped[j : j + 1]

    def send(there, other):
        pltpu.make_async_remote_copy(
            src_ref=parcel.at[other], dst_ref=inbox.at[me],
            send_sem=parcel_send, recv_sem=parcel_recv, device_id=there, device_id_type=MESH,
        ).start()

    each_other(send)
    keep = pltpu.make_async_copy(parcel.at[me], inbox.at[me], own)
    keep.start()
    keep.wait()
    for sem in (parcel_recv, parcel_send):
        pltpu.make_async_copy(
            inbox.at[pl.ds(0, total - 1)], inbox.at[pl.ds(0, total - 1)], sem
        ).wait()
    pltpu.make_async_copy(
        notes.at[pl.ds(0, total - 1)], notes.at[pl.ds(0, total - 1)], note_send
    ).wait()


def gather_kernel(inbox, vel_ref, grad_ref, final):
    total = inbox.shape[0]
    cells, slots = grad_ref.shape[:2]
    held = cells * slots
    parts = [inbox[other] for other in range(total)]
    while len(parts) > 1:
        parts = [a + b for a, b in zip(parts[0::2], parts[1::2])] + parts[len(parts) // 2 * 2 :]
    result = parts[0]
    for o in range(3):
        for s in range(slots):
            low = o * held + s * cells
            vel_ref[o, s : s + 1, :] = result[:, low : low + cells]
    final[...] = jnp.zeros_like(final)
    for h in range(2):
        final[h : h + 1, :] = result[:, h * LANES : (h + 1) * LANES]
    ends = final[...].T
    lane = lax.broadcasted_iota(jnp.int32, (cells, LANES), 1)
    for s in range(slots):
        table = jnp.zeros((cells, LANES), jnp.float32)
        for o in range(3, 12):
            low = (o % SUB) * held + s * cells
            column = ends[low : low + cells, o // SUB : o // SUB + 1]
            table = jnp.where(lane == o - 3, jnp.broadcast_to(column, (cells, LANES)), table)
        for c in range(cells):
            grad_ref[c, s : s + 1, :] = table[c : c + 1, 0:9]


def per_device(band_cells, cell_counts, cell_assign, wake_pos, wake_strength, wake_core):
    grid_rows = lax.axis_size("row")
    grid_cols = lax.axis_size("col")
    total = grid_rows * grid_cols
    cells, slots = band_cells.shape[1:]
    span = wake_pos.shape[1]
    width = -(-4 * cells * grid_cols // LANES) * LANES
    targets = total * cells * slots
    f32 = jnp.float32
    vmem = pl.BlockSpec(memory_space=pltpu.VMEM)
    hbm = pl.BlockSpec(memory_space=pltpu.HBM)
    bf16 = jnp.bfloat16
    i32 = jnp.int32
    inbox = pl.pallas_call(
        functools.partial(kernel, grid_rows, grid_cols),
        out_shape=jax.ShapeDtypeStruct((total, 1, 2 * LANES), f32),
        in_specs=[hbm] * 6,
        out_specs=hbm,
        scratch_shapes=[
            pltpu.SMEM((3, slots, cells), f32),
            pltpu.SMEM((cells,), i32),
            pltpu.SMEM((cells,), i32),
            pltpu.VMEM((3, span), f32),
            pltpu.VMEM((3, span), f32),
            pltpu.VMEM((1, span), f32),
            pltpu.SemaphoreType.DMA((6,)),
            pltpu.VMEM((ROWS, 2 * CHUNK), bf16),
            pltpu.VMEM((ROWS, 2 * CHUNK), bf16),
            pltpu.VMEM((1, 1, slots * width), f32),
            pltpu.VMEM((total, 1, slots * width), f32),
            pltpu.VMEM((LANES, width), f32),
            pltpu.VMEM((4, targets, LANES), f32),
            pltpu.VMEM((targets, LANES), bf16),
            pltpu.VMEM((DEPTH, span), bf16),
            pltpu.VMEM((LANES, span), jnp.bfloat16),
            pltpu.VMEM((targets, LANES), f32),
            pltpu.VMEM((total, 1, 2 * LANES), f32),
            pltpu.SemaphoreType.DMA,
            pltpu.SemaphoreType.DMA,
            pltpu.SemaphoreType.DMA,
            pltpu.SemaphoreType.DMA,
            pltpu.SemaphoreType.DMA,
        ],
        compiler_params=pltpu.CompilerParams(
            collective_id=0, has_side_effects=True, vmem_limit_bytes=60 * 1024 * 1024
        ),
        name="wake_sums",
    )(band_cells.transpose(0, 2, 1), cell_counts, cell_assign, wake_pos, wake_strength, wake_core)
    velocity, gradient = pl.pallas_call(
        gather_kernel,
        out_shape=(
            jax.ShapeDtypeStruct((3, slots, cells), f32),
            jax.ShapeDtypeStruct((cells, slots, 9), f32),
        ),
        in_specs=[vmem],
        out_specs=(vmem, vmem),
        scratch_shapes=[pltpu.VMEM((LANES, LANES), f32)],
        name="last_sum",
    )(inbox)
    return velocity.transpose(0, 2, 1), gradient.transpose(2, 0, 1)


def solution(mesh):
    placed = (
        P(None, ("row", "col"), None),
        P(("row", "col")),
        P(("row", "col")),
        P(None, ("row", "col")),
        P(None, ("row", "col")),
        P(None, ("row", "col")),
    )
    return jax.shard_map(
        per_device,
        mesh=mesh,
        in_specs=placed,
        out_specs=(P(None, ("row", "col"), None), P(None, ("row", "col"), None)),
        check_vma=False,
    )
```

time: 150 us -> 29.3 us (0.20)
  blocking collectives: 58.3 us -> 0 us
  other arithmetic: 48.7 us -> 0 us
  Pallas kernels: 0 us -> 28.5 us
  waiting for transfers between devices: 16 us -> 0 us
  between operations: 14.8 us -> 0.64 us
  local copies, waits for them, and re-layouts: 8.47 us -> 0 us
  loops' own time: 2.78 us -> 0 us
    all_gather x4 -> x0, blocking collectives: 44.9 us -> none  [the longest x1 13.1 us: per_device(): lax.all_gather(band_cells, 'col', axis=1, tiled=True)]
    reduce_sum x4 -> x0, other arithmetic: 44.2 us -> none  [block_sums(): return jnp.stack([jnp.sum(term, axis=1) for term in terms_list])]
    pallas_call x0 -> x2, Pallas kernels: none -> 28.5 us  [the longest x1 26.9 us: per_device(): pl.pallas_call(functools.partial(kernel, grid_rows, grid_cols), out_shape...]
    unnamed x2 -> x0, waiting for transfers between devices: 16 us -> none
    unnamed x1 -> x0, blocking collectives: 13.4 us -> none
    unnamed x8 -> x0, local copies, waits for them, and re-layouts: 3.38 us -> none
    another operation x1 -> x0, loops' own time: 2.78 us -> none  [pair_sums(): lax.scan(one_block, start_sums, jnp.arange(block_steps, dtype=jnp.int32))]
    dynamic_slice x5 -> x0, local copies, waits for them, and re-layouts: 2.43 us -> none  [the longest x4 2.34 us: pair_sums(): lax.scan(one_block, start_sums, jnp.arange(block_steps, dtype=jnp.int32))]
  transfers between devices with their start and end apart: 1 -> 0, of which waited for: 1 -> 0; matrix products, arithmetic and copies ran while one was open for 0% -> 0% of each run, Pallas kernels for 0% -> 0%
where the time goes in v1:
time: 29.3 us; the launch traced here: 29.1 us
  Pallas kernels  28.5 us (97%)
  between operations  0.64 us (2%)
    pallas_call x1, Pallas kernels, per_device(): pl.pallas_call(functools.partial(kernel, grid_rows, grid_cols), out_shape...  26.9 us
    pallas_call x1, Pallas kernels, per_device(): pl.pallas_call(gather_kernel, out_shape=(jax.ShapeDtypeStruct((3, slots,...  1.57 us

profile of v1, /device:TPU:0, one launch (start us, length us, event | category | flops | bytes accessed | tf_op | source)
XLA Modules:
  0.0 29.1 jit_solution(8308929603552729316)
XLA Ops:
  0.6 26.9 %wake_sums.1.inbox = f32[32,1,256]{2,1,0:T(1,128)} custom-call(f32[3,2,8]{2,1,0:T(2,128)} %bitcast.3, s32[8]{0:T(128)} %counts_hbm.1, s32[8]{0:T(128)} %assign_hbm.1, f32[3,8192]{1,0:T(4,128)} %pos_hbm.1, f32[3,8192]{1,0:T(4,128)} %str_hbm.1, f32[1,8192]{1,0:T(1,128)} %core_hbm.1), custom_call_target="tpu_custom_call" | custom-call | tf_op jit(solution)/shard_map/wake_sums/pallas_call | solution.py:346
  27.5 1.6 %last_sum.1 = (f32[3,2,8]{2,1,0:T(2,128)}, f32[8,2,9]{2,1,0:T(2,128)}) custom-call(f32[32,1,256]{2,1,0:T(1,128)} %wake_sums.1.inbox), custom_call_target="tpu_custom_call" | custom-call | tf_op jit(solution)/shard_map/last_sum/pallas_call | solution.py:381

commit v2 on v1

--- a/solution.py
+++ b/solution.py
@@ -11,7 +11,7 @@
 MESH = pl.DeviceIdType.MESH
 LANES = 128
 SUB = 8
-CHUNK = 512
+CHUNK = 1024
 PREPARE = 1024
 ROWS = 512
 STRIP = 32
@@ -97,17 +97,6 @@
             value = jnp.where(kind == k, columns[k][s] - CENTRE, value)
         value = jnp.where(chosen, value, 0.0)
         note[0, :, s * width : (s + 1) * width] = jnp.sum(value, axis=0, keepdims=True)
-
-    pl.semaphore_wait(barrier, total - 1)
-
-    def tell(there, other):
-        pltpu.make_async_remote_copy(
-            src_ref=note.at[0], dst_ref=notes.at[me], send_sem=note_send, recv_sem=note_recv,
-            device_id=there, device_id_type=MESH,
-        ).start()
-
-    each_other(tell)
-    notes[me] = note[0]
 
     for one in fetches[3:]:
         one.wait()
@@ -138,7 +127,21 @@
         weights[:, cols] = jnp.concatenate(rows, axis=0).astype(jnp.bfloat16)
         return unused
 
-    lax.fori_loop(0, span // PREPARE, prepare, 0)
+    ahead = span // PREPARE // 2
+    lax.fori_loop(0, ahead, prepare, 0)
+
+    pl.semaphore_wait(barrier, total - 1)
+
+    def tell(there, other):
+        pltpu.make_async_remote_copy(
+            src_ref=note.at[0], dst_ref=notes.at[me], send_sem=note_send, recv_sem=note_recv,
+            device_id=there, device_id_type=MESH,
+        ).start()
+
+    each_other(tell)
+    notes[me] = note[0]
+
+    lax.fori_loop(ahead, span // PREPARE, prepare, 0)
 
     pltpu.make_async_copy(
         notes.at[pl.ds(0, total - 1)], notes.at[pl.ds(0, total - 1)], note_recv
@@ -193,13 +196,15 @@
         first = lax.rem(index, parts) * ROWS
         return cols, first
 
-    def powers(index, store):
+    def radii(index):
         cols, first = where_at(index)
 
         rows = pl.ds(pl.multiple_of(first, ROWS), ROWS)
-        radius = jnp.dot(
+        return jnp.dot(
             left[rows, 0:DEPTH], source[:, cols], preferred_element_type=jnp.float32
         )
+
+    def powers(radius, store):
         for low in range(0, ROWS, STRIP):
             inverse = lax.rsqrt(radius[low : low + STRIP])
             square = inverse * inverse
@@ -217,19 +222,22 @@
             store[...], both, (((1,), (1,)), ((), ())), preferred_element_type=jnp.float32
         )
 
-    powers(0, even)
+    powers(radii(0), even)
 
     def pairs(count, unused):
         index = 2 * count
+        radius = radii(index + 1)
         add(index, even)
-        powers(index + 1, odd)
+        powers(radius, odd)
+        radius = radii(index + 2)
         add(index + 1, odd)
-        powers(index + 2, even)
+        powers(radius, even)
         return unused
 
     lax.fori_loop(0, steps // 2 - 1, pairs, 0)
+    radius = radii(steps - 1)
     add(steps - 2, even)
-    powers(steps - 1, odd)
+    powers(radius, odd)
     add(steps - 1, odd)
 
     scale = -1.0 / (4.0 * math.pi)

time: 29.3 us -> 28.1 us (0.959)
  Pallas kernels: 28.5 us -> 27.2 us
    pallas_call x1, Pallas kernels: 26.9 us -> 25.6 us  [per_device(): pl.pallas_call(functools.partial(kernel, grid_rows, grid_cols), out_shape...]
where the time goes in v2:
time: 28.1 us; the launch traced here: 27.8 us
  Pallas kernels  27.2 us (97%)
  between operations  0.64 us (2%)
    pallas_call x1, Pallas kernels, per_device(): pl.pallas_call(functools.partial(kernel, grid_rows, grid_cols), out_shape...  25.6 us
    pallas_call x1, Pallas kernels, per_device(): pl.pallas_call(gather_kernel, out_shape=(jax.ShapeDtypeStruct((3, slots,...  1.57 us

profile of v2, /device:TPU:0, one launch (start us, length us, event | category | flops | bytes accessed | tf_op | source)
XLA Modules:
  0.0 27.8 jit_solution(7727680127713280027)
XLA Ops:
  0.6 25.6 %wake_sums.1.inbox = f32[32,1,256]{2,1,0:T(1,128)} custom-call(f32[3,2,8]{2,1,0:T(2,128)} %bitcast.3, s32[8]{0:T(128)} %counts_hbm.1, s32[8]{0:T(128)} %assign_hbm.1, f32[3,8192]{1,0:T(4,128)} %pos_hbm.1, f32[3,8192]{1,0:T(4,128)} %str_hbm.1, f32[1,8192]{1,0:T(1,128)} %core_hbm.1), custom_call_target="tpu_custom_call" | custom-call | tf_op jit(solution)/shard_map/wake_sums/pallas_call | solution.py:354
  26.3 1.6 %last_sum.1 = (f32[3,2,8]{2,1,0:T(2,128)}, f32[8,2,9]{2,1,0:T(2,128)}) custom-call(f32[32,1,256]{2,1,0:T(1,128)} %wake_sums.1.inbox), custom_call_target="tpu_custom_call" | custom-call | tf_op jit(solution)/shard_map/last_sum/pallas_call | solution.py:389
